TPU v7x, 32 devices: a whole 2x2x4 slice. The times are simulated.
32 devices in a mesh: groups: 2 (over x), blk: 8 (over z, y), inner: 2 (over core).
Axes of the slice: x: 2, y: 2, z: 4, core: 2. Of those that a mesh axis runs over, the one named last changes fastest.
Arguments:
- embeddings: bfloat16 [16384, 1024], P(('groups', 'blk', 'inner')), parts along dimension 0, may hold values from -30 to 30
- cluster_ids: int32 [16384], P(('groups', 'blk', 'inner')), parts along dimension 0, may hold values from 0 to 15
- live_rows: int32 [32], P(('groups', 'blk', 'inner')), parts along dimension 0, may hold values from 1 to 512, 6144 in all
Outputs:
- weights: float32 [16384], P(('groups', 'blk', 'inner')), parts along dimension 0
There are 2 independent parts, one for each index of `groups`. A program takes and returns all parts, laid end to end along the dimension named above; each array names one. Nothing has to cross between parts.
Inputs may be any that keep to these rules, and one draw needn't show every extreme that they name: `live_rows`: some shard is full.
All inputs are finite; a program needn't handle non-finite values.
Results may differ from a plain program's by a relative error of at most 0.0047.
Values may be sent and summed in bfloat16 or wider, within the bound.
A program may use at most 64 MiB of HBM per device.

v0:
```python
import math

import jax
import jax.numpy as jnp
from jax import lax
from jax.sharding import PartitionSpec as P

sharpness = 8.0
cross_weight = 0.25
base_weight = 8.0
epsilon = 1e-06


def as_sent(value):

    def short(part):
        return part.astype(jnp.bfloat16) if part.dtype == jnp.float32 else part

    return jax.tree.map(short, value)


def from_behind(block, axis, distance):
    devices = range(lax.axis_size(axis))
    route = [((i - distance) % len(devices), i) for i in devices]
    return lax.ppermute(block, axis, route)


def normalize(embeddings):
    widened = embeddings.astype(jnp.float32)
    scaled = lax.rsqrt(jnp.mean(widened * widened, axis=1, keepdims=True) + epsilon) / math.sqrt(
        widened.shape[1]
    )
    return (widened * scaled).astype(jnp.bfloat16)


def kernel_tile(unit_rows, row_tags, visible_rows, visible_tags):
    cosines = lax.dot_general(
        unit_rows, visible_rows, (((1,), (1,)), ((), ())), preferred_element_type=jnp.float32
    )
    own_mask = (row_tags >= 0).astype(jnp.float32)
    seen_mask = (visible_tags >= 0).astype(jnp.float32)
    weighting = jnp.where(row_tags[:, None] == visible_tags[None, :], 1.0, cross_weight)
    weighting = weighting * own_mask[:, None] * seen_mask[None, :]
    return jnp.exp(sharpness * (cosines - 1.0)) * weighting


def body(embeddings, cluster_ids, live_rows):
    row_count = embeddings.shape[0]
    unit_rows = normalize(embeddings)
    position = lax.broadcasted_iota(jnp.int32, (row_count,), 0)
    row_tags = jnp.where(position < live_rows[0], cluster_ids, -1)
    own_block = (unit_rows, row_tags)
    cycle_size = lax.axis_size("blk")

    def advance(visitor):
        return jax.tree.map(
            lambda part, own: part.astype(own.dtype),
            from_behind(as_sent(visitor), "blk", 1),
            visitor,
        )

    def widen_block(visitor):
        return jax.tree.map(
            lambda part, own: part.astype(own.dtype),
            lax.all_gather(as_sent(visitor), "inner", axis=0, tiled=True),
            visitor,
        )

    visible = widen_block(own_block)
    row_total = jnp.sum(kernel_tile(unit_rows, row_tags, visible[0], visible[1]), axis=1)

    def full_step(turn_index, carried):
        visitor, running = carried
        visitor = advance(visitor)
        seen_block = widen_block(visitor)
        kernel = kernel_tile(unit_rows, row_tags, seen_block[0], seen_block[1])
        return (visitor, running + jnp.sum(kernel, axis=1))

    visitor, row_total = lax.fori_loop(1, cycle_size, full_step, (own_block, row_total))
    row_mask = (row_tags >= 0).astype(jnp.float32)
    return row_mask * base_weight / (row_total + 1.0 - row_mask)


def solution(mesh):
    return jax.shard_map(
        body,
        mesh=mesh,
        in_specs=(
            P(("groups", "blk", "inner"), None),
            P(("groups", "blk", "inner")),
            P(("groups", "blk", "inner")),
        ),
        out_specs=P(("groups", "blk", "inner")),
        check_vma=False,
    )
```

profile of v0, /device:TPU:0, one launch (start us, length us, event | category | flops | bytes accessed | tf_op | source)
XLA Modules:
  0.0 326.6 jit_solution(15632848854520047122)
XLA Ops:
  8.1 2.5 fusion.1
  12.5 1.9 all-gather.1
  14.5 9.5 %all-gather.7.cloned.1.call-done = bf16[1024,1024]{1,0:T(8,128)(2,1)} async-done(((bf16[512,1024]{1,0:T(8,128)(2,1)}), bf16[1024,1024]{1,0:T(8,128)(2,1)}) %all-gather.7.cloned.1.call-update) | async-done | bytes 2097168 | tf_op jit(solution)/shard_map/all_gather | solution.py:65
  24.0 3.2 multiply_reduce_fusion.1
  27.2 291.9 %while.16 = (s32[]{:T(128)}, bf16[512,1024]{1,0:T(8,128)(2,1)S(1)}, s32[512]{0:T(512)S(1)}, f32[512]{0:T(512)S(1)}, bf16[512,1024]{1,0:T(8,128)(2,1)S(1)}, /*index=5*/s32[512]{0:T(512)S(1)}, s32[]{:T(128)}) while((s32[]{:T(128)}, bf16[512,1024]{1,0:T(8,128)(2,1)S(1)}, s32[512]{0:T(512)S(1)}, f32[512]{0:T(512)S(1)}, ...), condition=%wide.region_4.5_spmd, body=%wide.region_2.4_spmd.sunk | while | flops 1077939200 | bytes 23120096 | solution.py:79
  27.3 1.8 collective-permute-start
  29.0 26.4 %collective-permute-done = bf16[512,1024]{1,0:T(8,128)(2,1)S(1)} collective-permute-done((bf16[512,1024]{1,0:T(8,128)(2,1)S(1)}, bf16[512,1024]{1,0:T(8,128)(2,1)S(1)}, u32[]{:S(2)}, u32[]{:S(2)}) %collective-permute-start) | collective-permute-done | bytes 1048608 | tf_op jit(solution)/shard_map/while/body/eval_jaxpr/ppermute | solution.py:25
  56.5 6.3 %collective-permute-done.1 = s32[512]{0:T(512)S(1)} collective-permute-done((s32[512]{0:T(512)S(1)}, s32[512]{0:T(512)S(1)}, u32[]{:S(2)}, u32[]{:S(2)}) %collective-permute-start.1) | collective-permute-done | bytes 2080 | tf_op jit(solution)/shard_map/while/body/eval_jaxpr/ppermute | solution.py:25
  62.8 1.8 all-gather.3
  65.8 3.2 multiply_reduce_fusion.3
  70.7 26.4 %collective-permute-done = bf16[512,1024]{1,0:T(8,128)(2,1)S(1)} collective-permute-done((bf16[512,1024]{1,0:T(8,128)(2,1)S(1)}, bf16[512,1024]{1,0:T(8,128)(2,1)S(1)}, u32[]{:S(2)}, u32[]{:S(2)}) %collective-permute-start) | collective-permute-done | bytes 1048608 | tf_op jit(solution)/shard_map/while/body/eval_jaxpr/ppermute | solution.py:25
  98.2 6.3 %collective-permute-done.1 = s32[512]{0:T(512)S(1)} collective-permute-done((s32[512]{0:T(512)S(1)}, s32[512]{0:T(512)S(1)}, u32[]{:S(2)}, u32[]{:S(2)}) %collective-permute-start.1) | collective-permute-done | bytes 2080 | tf_op jit(solution)/shard_map/while/body/eval_jaxpr/ppermute | solution.py:25
  107.5 3.2 multiply_reduce_fusion.3
  112.3 26.5 %collective-permute-done = bf16[512,1024]{1,0:T(8,128)(2,1)S(1)} collective-permute-done((bf16[512,1024]{1,0:T(8,128)(2,1)S(1)}, bf16[512,1024]{1,0:T(8,128)(2,1)S(1)}, u32[]{:S(2)}, u32[]{:S(2)}) %collective-permute-start) | collective-permute-done | bytes 1048608 | tf_op jit(solution)/shard_map/while/body/eval_jaxpr/ppermute | solution.py:25
  139.9 6.3 %collective-permute-done.1 = s32[512]{0:T(512)S(1)} collective-permute-done((s32[512]{0:T(512)S(1)}, s32[512]{0:T(512)S(1)}, u32[]{:S(2)}, u32[]{:S(2)}) %collective-permute-start.1) | collective-permute-done | bytes 2080 | tf_op jit(solution)/shard_map/while/body/eval_jaxpr/ppermute | solution.py:25
  146.2 1.8 all-gather.3
  149.2 3.2 multiply_reduce_fusion.3
  154.0 26.5 %collective-permute-done = bf16[512,1024]{1,0:T(8,128)(2,1)S(1)} collective-permute-done((bf16[512,1024]{1,0:T(8,128)(2,1)S(1)}, bf16[512,1024]{1,0:T(8,128)(2,1)S(1)}, u32[]{:S(2)}, u32[]{:S(2)}) %collective-permute-start) | collective-permute-done | bytes 1048608 | tf_op jit(solution)/shard_map/while/body/eval_jaxpr/ppermute | solution.py:25
  181.6 6.3 %collective-permute-done.1 = s32[512]{0:T(512)S(1)} collective-permute-done((s32[512]{0:T(512)S(1)}, s32[512]{0:T(512)S(1)}, u32[]{:S(2)}, u32[]{:S(2)}) %collective-permute-start.1) | collective-permute-done | bytes 2080 | tf_op jit(solution)/shard_map/while/body/eval_jaxpr/ppermute | solution.py:25
  187.8 1.8 all-gather.3
  190.8 3.2 multiply_reduce_fusion.3
  195.6 26.6 %collective-permute-done = bf16[512,1024]{1,0:T(8,128)(2,1)S(1)} collective-permute-done((bf16[512,1024]{1,0:T(8,128)(2,1)S(1)}, bf16[512,1024]{1,0:T(8,128)(2,1)S(1)}, u32[]{:S(2)}, u32[]{:S(2)}) %collective-permute-start) | collective-permute-done | bytes 1048608 | tf_op jit(solution)/shard_map/while/body/eval_jaxpr/ppermute | solution.py:25
  223.3 6.3 %collective-permute-done.1 = s32[512]{0:T(512)S(1)} collective-permute-done((s32[512]{0:T(512)S(1)}, s32[512]{0:T(512)S(1)}, u32[]{:S(2)}, u32[]{:S(2)}) %collective-permute-start.1) | collective-permute-done | bytes 2080 | tf_op jit(solution)/shard_map/while/body/eval_jaxpr/ppermute | solution.py:25
  229.5 1.8 all-gather.3
  232.5 3.2 multiply_reduce_fusion.3
  237.3 26.6 %collective-permute-done = bf16[512,1024]{1,0:T(8,128)(2,1)S(1)} collective-permute-done((bf16[512,1024]{1,0:T(8,128)(2,1)S(1)}, bf16[512,1024]{1,0:T(8,128)(2,1)S(1)}, u32[]{:S(2)}, u32[]{:S(2)}) %collective-permute-start) | collective-permute-done | bytes 1048608 | tf_op jit(solution)/shard_map/while/body/eval_jaxpr/ppermute | solution.py:25
  265.0 6.3 %collective-permute-done.1 = s32[512]{0:T(512)S(1)} collective-permute-done((s32[512]{0:T(512)S(1)}, s32[512]{0:T(512)S(1)}, u32[]{:S(2)}, u32[]{:S(2)}) %collective-permute-start.1) | collective-permute-done | bytes 2080 | tf_op jit(solution)/shard_map/while/body/eval_jaxpr/ppermute | solution.py:25
  274.2 3.2 multiply_reduce_fusion.3
  278.9 26.6 %collective-permute-done = bf16[512,1024]{1,0:T(8,128)(2,1)S(1)} collective-permute-done((bf16[512,1024]{1,0:T(8,128)(2,1)S(1)}, bf16[512,1024]{1,0:T(8,128)(2,1)S(1)}, u32[]{:S(2)}, u32[]{:S(2)}) %collective-permute-start) | collective-permute-done | bytes 1048608 | tf_op jit(solution)/shard_map/while/body/eval_jaxpr/ppermute | solution.py:25
  306.6 6.3 %collective-permute-done.1 = s32[512]{0:T(512)S(1)} collective-permute-done((s32[512]{0:T(512)S(1)}, s32[512]{0:T(512)S(1)}, u32[]{:S(2)}, u32[]{:S(2)}) %collective-permute-start.1) | collective-permute-done | bytes 2080 | tf_op jit(solution)/shard_map/while/body/eval_jaxpr/ppermute | solution.py:25
  312.9 1.8 all-gather.3
  315.9 3.2 multiply_reduce_fusion.3
  (98 shorter events, 32.4 us)
Async XLA Ops:
  6.5 17.4 %all-gather.7.cloned.1.call-start = ((), (), s32[]{:S(2)}) async-start(), calls=%async_computation | async-start | bytes 3145728 | tf_op jit(solution)/shard_map/all_gather | solution.py:65
  10.5 2.0 copy-start.2
  10.5 13.5 %copy-start.1 = (bf16[512,1024]{1,0:T(8,128)(2,1)S(1)}, bf16[512,1024]{1,0:T(8,128)(2,1)}, u32[]{:S(2)}) copy-start(bf16[512,1024]{1,0:T(8,128)(2,1)} %fusion.1) | copy-start | bytes 3145732
  27.2 38.6 %all-gather.9.cloned.1.call-start = ((), (), s32[]{:S(2)}) async-start(), calls=%async_computation.1 | async-start | bytes 3145728 | tf_op jit(solution)/shard_map/while/body/eval_jaxpr/all_gather | solution.py:65
  27.3 28.2 %collective-permute-start = (bf16[512,1024]{1,0:T(8,128)(2,1)S(1)}, bf16[512,1024]{1,0:T(8,128)(2,1)S(1)}, u32[]{:S(2)}, u32[]{:S(2)}) collective-permute-start(bf16[512,1024]{1,0:T(8,128)(2,1)S(1)} %get-tuple-element.143), channel_id=1, source_target_pairs={{14,0},{0,2},{2,4},{4,6},{6,8},{8,10},{10,12},{12,14},{15,1},{1,3}... | collective-permute-start | bytes 3145736 | tf_op jit(solution)/shard_map/while/body/eval_jaxpr/ppermute | solution.py:25
  55.4 1.0 copy-start
  56.5 6.3 %collective-permute-start.1 = (s32[512]{0:T(512)S(1)}, s32[512]{0:T(512)S(1)}, u32[]{:S(2)}, u32[]{:S(2)}) collective-permute-start(s32[512]{0:T(512)S(1)} %get-tuple-element.144), channel_id=1, source_target_pairs={{14,0},{0,2},{2,4},{4,6},{6,8},{8,10},{10,12},{12,14},{15,1},{1,3}... | collective-permute-start | bytes 6152 | tf_op jit(solution)/shard_map/while/body/eval_jaxpr/ppermute | solution.py:25
  69.1 38.4 %all-gather.9.cloned.1.call-start = ((), (), s32[]{:S(2)}) async-start(), calls=%async_computation.1 | async-start | bytes 3145728 | tf_op jit(solution)/shard_map/while/body/eval_jaxpr/all_gather | solution.py:65
  69.1 28.0 %collective-permute-start = (bf16[512,1024]{1,0:T(8,128)(2,1)S(1)}, bf16[512,1024]{1,0:T(8,128)(2,1)S(1)}, u32[]{:S(2)}, u32[]{:S(2)}) collective-permute-start(bf16[512,1024]{1,0:T(8,128)(2,1)S(1)} %get-tuple-element.143), channel_id=1, source_target_pairs={{14,0},{0,2},{2,4},{4,6},{6,8},{8,10},{10,12},{12,14},{15,1},{1,3}... | collective-permute-start | bytes 3145736 | tf_op jit(solution)/shard_map/while/body/eval_jaxpr/ppermute | solution.py:25
  97.1 1.0 copy-start
  98.1 6.3 %collective-permute-start.1 = (s32[512]{0:T(512)S(1)}, s32[512]{0:T(512)S(1)}, u32[]{:S(2)}, u32[]{:S(2)}) collective-permute-start(s32[512]{0:T(512)S(1)} %get-tuple-element.144), channel_id=1, source_target_pairs={{14,0},{0,2},{2,4},{4,6},{6,8},{8,10},{10,12},{12,14},{15,1},{1,3}... | collective-permute-start | bytes 6152 | tf_op jit(solution)/shard_map/while/body/eval_jaxpr/ppermute | solution.py:25
  110.7 38.4 %all-gather.9.cloned.1.call-start = ((), (), s32[]{:S(2)}) async-start(), calls=%async_computation.1 | async-start | bytes 3145728 | tf_op jit(solution)/shard_map/while/body/eval_jaxpr/all_gather | solution.py:65
  110.8 28.0 %collective-permute-start = (bf16[512,1024]{1,0:T(8,128)(2,1)S(1)}, bf16[512,1024]{1,0:T(8,128)(2,1)S(1)}, u32[]{:S(2)}, u32[]{:S(2)}) collective-permute-start(bf16[512,1024]{1,0:T(8,128)(2,1)S(1)} %get-tuple-element.143), channel_id=1, source_target_pairs={{14,0},{0,2},{2,4},{4,6},{6,8},{8,10},{10,12},{12,14},{15,1},{1,3}... | collective-permute-start | bytes 3145736 | tf_op jit(solution)/shard_map/while/body/eval_jaxpr/ppermute | solution.py:25
  138.8 1.0 copy-start
  139.8 6.3 %collective-permute-start.1 = (s32[512]{0:T(512)S(1)}, s32[512]{0:T(512)S(1)}, u32[]{:S(2)}, u32[]{:S(2)}) collective-permute-start(s32[512]{0:T(512)S(1)} %get-tuple-element.144), channel_id=1, source_target_pairs={{14,0},{0,2},{2,4},{4,6},{6,8},{8,10},{10,12},{12,14},{15,1},{1,3}... | collective-permute-start | bytes 6152 | tf_op jit(solution)/shard_map/while/body/eval_jaxpr/ppermute | solution.py:25
  152.4 38.4 %all-gather.9.cloned.1.call-start = ((), (), s32[]{:S(2)}) async-start(), calls=%async_computation.1 | async-start | bytes 3145728 | tf_op jit(solution)/shard_map/while/body/eval_jaxpr/all_gather | solution.py:65
  152.5 28.0 %collective-permute-start = (bf16[512,1024]{1,0:T(8,128)(2,1)S(1)}, bf16[512,1024]{1,0:T(8,128)(2,1)S(1)}, u32[]{:S(2)}, u32[]{:S(2)}) collective-permute-start(bf16[512,1024]{1,0:T(8,128)(2,1)S(1)} %get-tuple-element.143), channel_id=1, source_target_pairs={{14,0},{0,2},{2,4},{4,6},{6,8},{8,10},{10,12},{12,14},{15,1},{1,3}... | collective-permute-start | bytes 3145736 | tf_op jit(solution)/shard_map/while/body/eval_jaxpr/ppermute | solution.py:25
  180.5 1.0 copy-start
  181.5 6.3 %collective-permute-start.1 = (s32[512]{0:T(512)S(1)}, s32[512]{0:T(512)S(1)}, u32[]{:S(2)}, u32[]{:S(2)}) collective-permute-start(s32[512]{0:T(512)S(1)} %get-tuple-element.144), channel_id=1, source_target_pairs={{14,0},{0,2},{2,4},{4,6},{6,8},{8,10},{10,12},{12,14},{15,1},{1,3}... | collective-permute-start | bytes 6152 | tf_op jit(solution)/shard_map/while/body/eval_jaxpr/ppermute | solution.py:25
  194.1 38.4 %all-gather.9.cloned.1.call-start = ((), (), s32[]{:S(2)}) async-start(), calls=%async_computation.1 | async-start | bytes 3145728 | tf_op jit(solution)/shard_map/while/body/eval_jaxpr/all_gather | solution.py:65
  194.2 28.0 %collective-permute-start = (bf16[512,1024]{1,0:T(8,128)(2,1)S(1)}, bf16[512,1024]{1,0:T(8,128)(2,1)S(1)}, u32[]{:S(2)}, u32[]{:S(2)}) collective-permute-start(bf16[512,1024]{1,0:T(8,128)(2,1)S(1)} %get-tuple-element.143), channel_id=1, source_target_pairs={{14,0},{0,2},{2,4},{4,6},{6,8},{8,10},{10,12},{12,14},{15,1},{1,3}... | collective-permute-start | bytes 3145736 | tf_op jit(solution)/shard_map/while/body/eval_jaxpr/ppermute | solution.py:25
  222.2 1.0 copy-start
  223.2 6.3 %collective-permute-start.1 = (s32[512]{0:T(512)S(1)}, s32[512]{0:T(512)S(1)}, u32[]{:S(2)}, u32[]{:S(2)}) collective-permute-start(s32[512]{0:T(512)S(1)} %get-tuple-element.144), channel_id=1, source_target_pairs={{14,0},{0,2},{2,4},{4,6},{6,8},{8,10},{10,12},{12,14},{15,1},{1,3}... | collective-permute-start | bytes 6152 | tf_op jit(solution)/shard_map/while/body/eval_jaxpr/ppermute | solution.py:25
  235.8 38.4 %all-gather.9.cloned.1.call-start = ((), (), s32[]{:S(2)}) async-start(), calls=%async_computation.1 | async-start | bytes 3145728 | tf_op jit(solution)/shard_map/while/body/eval_jaxpr/all_gather | solution.py:65
  235.8 28.0 %collective-permute-start = (bf16[512,1024]{1,0:T(8,128)(2,1)S(1)}, bf16[512,1024]{1,0:T(8,128)(2,1)S(1)}, u32[]{:S(2)}, u32[]{:S(2)}) collective-permute-start(bf16[512,1024]{1,0:T(8,128)(2,1)S(1)} %get-tuple-element.143), channel_id=1, source_target_pairs={{14,0},{0,2},{2,4},{4,6},{6,8},{8,10},{10,12},{12,14},{15,1},{1,3}... | collective-permute-start | bytes 3145736 | tf_op jit(solution)/shard_map/while/body/eval_jaxpr/ppermute | solution.py:25
  263.9 1.0 copy-start
  264.9 6.3 %collective-permute-start.1 = (s32[512]{0:T(512)S(1)}, s32[512]{0:T(512)S(1)}, u32[]{:S(2)}, u32[]{:S(2)}) collective-permute-start(s32[512]{0:T(512)S(1)} %get-tuple-element.144), channel_id=1, source_target_pairs={{14,0},{0,2},{2,4},{4,6},{6,8},{8,10},{10,12},{12,14},{15,1},{1,3}... | collective-permute-start | bytes 6152 | tf_op jit(solution)/shard_map/while/body/eval_jaxpr/ppermute | solution.py:25
  277.5 38.4 %all-gather.9.cloned.1.call-start = ((), (), s32[]{:S(2)}) async-start(), calls=%async_computation.1 | async-start | bytes 3145728 | tf_op jit(solution)/shard_map/while/body/eval_jaxpr/all_gather | solution.py:65
  277.5 28.0 %collective-permute-start = (bf16[512,1024]{1,0:T(8,128)(2,1)S(1)}, bf16[512,1024]{1,0:T(8,128)(2,1)S(1)}, u32[]{:S(2)}, u32[]{:S(2)}) collective-permute-start(bf16[512,1024]{1,0:T(8,128)(2,1)S(1)} %get-tuple-element.143), channel_id=1, source_target_pairs={{14,0},{0,2},{2,4},{4,6},{6,8},{8,10},{10,12},{12,14},{15,1},{1,3}... | collective-permute-start | bytes 3145736 | tf_op jit(solution)/shard_map/while/body/eval_jaxpr/ppermute | solution.py:25
  305.5 1.0 copy-start
  306.6 6.3 %collective-permute-start.1 = (s32[512]{0:T(512)S(1)}, s32[512]{0:T(512)S(1)}, u32[]{:S(2)}, u32[]{:S(2)}) collective-permute-start(s32[512]{0:T(512)S(1)} %get-tuple-element.144), channel_id=1, source_target_pairs={{14,0},{0,2},{2,4},{4,6},{6,8},{8,10},{10,12},{12,14},{15,1},{1,3}... | collective-permute-start | bytes 6152 | tf_op jit(solution)/shard_map/while/body/eval_jaxpr/ppermute | solution.py:25
Sparse Core Ops, SparseCore 0:
  10.7 13.2 all-gather.6
  56.6 8.9 all-gather.8
  98.3 8.9 all-gather.8
  139.9 8.9 all-gather.8
  181.6 8.8 all-gather.8
  223.3 8.8 all-gather.8
  265.0 8.7 all-gather.8
  306.7 8.7 all-gather.8
where the time goes:
time: 327 us
  waiting for transfers between devices  239 us (73%)
  matrix products  25.9 us (8%)
  local copies, waits for them, and re-layouts  16.9 us (5%)
  blocking collectives  14.3 us (4%)
  between operations  14.1 us (4%)
  starting transfers between devices  11.4 us (3%)
  other arithmetic  4.71 us (1%)
    ppermute x14, waiting for transfers between devices, from_behind(): return lax.ppermute(block, axis, route)  229 us
    dot_general x8, matrix products, kernel_tile(): lax.dot_general(unit_rows, visible_rows, (((1,), (1,)), ((), ())), prefer...  25.9 us
    while x28, local copies, waits for them, and re-layouts  15.5 us
    all_gather x8, blocking collectives, widen_block(): lax.all_gather(as_sent(visitor), 'inner', axis=0, tiled=True)  14.3 us
    ppermute x14, starting transfers between devices, from_behind(): return lax.ppermute(block, axis, route)  11.1 us
    all_gather x8, waiting for transfers between devices, widen_block(): lax.all_gather(as_sent(visitor), 'inner', axis=0, tiled=True)  9.51 us
  transfers between devices with their start and end apart: 22, of which 15 were waited for; matrix products, arithmetic and copies ran while one was open for 3% of the time, Pallas kernels for 0%

commit v1 on v0

v1 whole, which is shorter than its diff:
```python
import functools
import math

import jax
import jax.numpy as jnp
from jax import lax
from jax.experimental import pallas as pl
from jax.experimental.pallas import tpu as pltpu
from jax.sharding import PartitionSpec as P

sharpness = 8.0
epsilon = 1e-06
base_weight = 8.0
MESH = pl.DeviceIdType.MESH
LOG2E = 1.4426950408889634
COLS = 2
QUAD = 2 * COLS
NEG = -1e30


def kernel(
    stages, chunks, emb, ids, live, out,
    quad, vis, tags, tag_col, cap_col, acc, vsum, rsum, gpart, gsum,
    fwd_send, own_send, vis_recv, y_send, y_recv, i_send, i_recv, d_send, d_recv,
    t_send, t_recv, r_send, r_recv, g_send, g_recv,
):
    rows, depth = emb.shape
    span = rows // chunks
    half = stages // 2 - 1
    blk, core = lax.axis_index("blk"), lax.axis_index("inner")
    stage, col = blk // COLS, blk % COLS
    upper = stage // (half + 1)
    q = col * 2 + core
    me = blk * 2 + core
    peers = stages * QUAD

    def at(s, y, c):
        return {"blk": s * COLS + y, "inner": c}

    def peer_of(index):
        return {"blk": index // 2, "inner": index % 2}

    def part(k):
        return pl.ds(pl.multiple_of(k * span, span), span)

    def remote(src, dst, send, recv, device):
        return pltpu.make_async_remote_copy(
            src_ref=src, dst_ref=dst, send_sem=send, recv_sem=recv,
            device_id=device, device_id_type=MESH,
        )

    def own_forward(k):
        return remote(quad.at[q, part(k)], vis.at[0, part(k)], own_send.at[k], vis_recv.at[0, k],
                      at(stage + 1, col, core))

    def own_back(k):
        return remote(quad.at[q, part(k)], vis.at[half + 1, part(k)], own_send.at[k],
                      vis_recv.at[half + 1, k], at(stage - 1, col, core))

    def pass_forward(s, k):
        slot = s + 1 - upper
        return remote(vis.at[s, part(k)], vis.at[slot, part(k)], fwd_send.at[s, k],
                      vis_recv.at[slot, k], at(stage + 1, col, core))

    def pass_back(s, k):
        slot = half + 1 + s
        return remote(vis.at[slot, part(k)], vis.at[slot + 1, part(k)], fwd_send.at[slot, k],
                      vis_recv.at[slot + 1, k], at(stage - 1, col, core))

    def arrival(slot, k):
        return remote(vis.at[slot, part(k)], vis.at[slot, part(k)], fwd_send.at[slot, k],
                      vis_recv.at[slot, k], at(stage, col, 1 - core))

    def across(owner, k):
        return remote(quad.at[owner, part(k)], quad.at[owner, part(k)], y_send.at[k], y_recv.at[k],
                      at(stage, 1 - col, core))

    def beside(owner, k):
        return remote(quad.at[owner, part(k)], quad.at[owner, part(k)], i_send.at[k], i_recv.at[k],
                      at(stage, col, 1 - core))

    def diagonal(owner, k):
        return remote(quad.at[owner, part(k)], quad.at[owner, part(k)], d_send.at[k], d_recv.at[k],
                      at(stage, col, 1 - core))

    def tag_copy(owner, sem, device):
        return remote(tags.at[owner], tags.at[owner], t_send.at[sem], t_recv.at[owner], device)

    q_across, q_beside = (1 - col) * 2 + core, col * 2 + 1 - core
    q_diag = (1 - col) * 2 + 1 - core

    barrier = pltpu.get_barrier_semaphore()

    def greet(p, _):
        pl.semaphore_signal(barrier, inc=1, device_id=peer_of((me + p) % peers), device_id_type=MESH)
        return 0

    lax.fori_loop(1, peers, greet, 0)

    def normalize(k):
        wide = emb[part(k), :].astype(jnp.float32)
        scale = lax.rsqrt(jnp.mean(wide * wide, axis=1, keepdims=True) + epsilon) / math.sqrt(depth)
        quad[q, part(k), :] = (wide * scale).astype(jnp.bfloat16)

    position = lax.broadcasted_iota(jnp.int32, (1, rows), 1)
    tags[me] = jnp.where(position < live[0], ids[...], -1).astype(jnp.float32)
    normalize(0)
    pl.semaphore_wait(barrier, peers - 1)

    def start_own(k):
        @pl.when(stage <= half)
        def _():
            own_forward(k).start()

        @pl.when(stage >= half + 2)
        def _():
            own_back(k).start()

        across(q, k).start()
        beside(q, k).start()

    def send_tags(p, _):
        tag_copy(me, p, peer_of((me + p) % peers)).start()
        return 0

    start_own(0)
    lax.fori_loop(1, peers, send_tags, 0)

    def rest(k, _):
        normalize(k)
        start_own(k)
        return 0

    lax.fori_loop(1, chunks, rest, 0)

    def receive(s, k):
        @pl.when(stage > s)
        def _():
            arrival(s, k).wait_recv()

            @pl.when(stage < stages - 1)
            def _():
                pass_forward(s, k).start()

        if s <= stages - 3 - half:
            @pl.when((stage > half) & (stage + s < stages - 1))
            def _():
                arrival(half + 1 + s, k).wait_recv()

                @pl.when(stage >= half + 2)
                def _():
                    pass_back(s, k).start()

    def first(k, _):
        receive(0, k)
        across(q_across, k).wait_recv()
        diagonal(q_across, k).start()
        return 0

    lax.fori_loop(0, chunks, first, 0)

    def take_tags(p, _):
        tag_copy((me + p) % peers, p, peer_of((me + p) % peers)).wait_recv()
        return 0

    lax.fori_loop(1, peers, take_tags, 0)
    for g in range(QUAD):
        row = tags[stage * QUAD + g]
        tall = jnp.broadcast_to(row, (128, rows)).T
        tag_col[g] = tall
        cap_col[g] = jnp.where(tall < 0, NEG, 0.0)
        acc[g] = jnp.zeros((rows, 128), jnp.float32)

    def settle(k, _):
        beside(q_beside, k).wait_recv()
        diagonal(q_diag, k).wait_recv()
        return 0

    lax.fori_loop(0, chunks, settle, 0)

    def visit(block, owner, slot, k, keep):
        seen = block[part(k), :]
        lanes = pl.ds(pl.multiple_of(k * span, span), span)
        tag_row = tags[owner, :, lanes]
        same = jnp.where(tag_row < 0, NEG, -sharpness * LOG2E)
        other = same - 2.0

        def tile(g, total):
            cosines = lax.dot_general(
                quad[g], seen, (((1,), (1,)), ((), ())), preferred_element_type=jnp.float32
            )
            bias = jnp.where(tag_col[g] == tag_row, same, other) + cap_col[g]
            weight = jnp.exp2(cosines * (sharpness * LOG2E) + bias)
            if keep:
                acc[g] += weight
            return total + jnp.sum(weight.reshape(rows // 8, 8, span), axis=0)

        total = lax.fori_loop(0, QUAD, tile, jnp.zeros((8, span), jnp.float32))
        vsum[slot, :, lanes] = jnp.sum(total, axis=0, keepdims=True)

    def owner_of(visitor):
        return visitor * QUAD + q

    def visit_forward(s, k):
        @pl.when((stage > s) & (stage <= half))
        def _():
            visit(vis.at[s], owner_of(stage - 1 - s), s, k, True)

        @pl.when(stage > half)
        def _():
            visit(vis.at[s], owner_of(half - s), s, k, True)

    def visit_back(s, k):
        if s <= stages - 3 - half:
            @pl.when((stage > half) & (stage + s < stages - 1))
            def _():
                visit(vis.at[half + 1 + s], owner_of(stage + 1 + s), half + 1 + s, k, True)

    for s in range(1, half + 1):
        def turn(k, _):
            if s == 1:
                visit(quad.at[q], me, stages - 1, k, False)
                visit_forward(0, k)
                visit_back(0, k)
            receive(s, k)
            visit_forward(s, k)
            visit_back(s, k)
            return 0

        lax.fori_loop(0, chunks, turn, 0)

    def give_back(slot, visitor):
        return remote(vsum.at[slot], rsum.at[stage], r_send.at[slot], r_recv.at[stage],
                      at(visitor, col, core))

    def each_return(act):
        for s in range(half + 1):
            @pl.when((stage > s) & (stage <= half))
            def _():
                act(give_back(s, stage - 1 - s))

            @pl.when(stage > half)
            def _():
                act(give_back(s, half - s))

            if s <= stages - 3 - half:
                @pl.when((stage > half) & (stage + s < stages - 1))
                def _():
                    act(give_back(half + 1 + s, stage + 1 + s))

    each_return(lambda copy: copy.start())
    for g in range(QUAD):
        gpart[g] = jnp.sum(acc[g].T, axis=0, keepdims=True)

    def share(step):
        g = (q + step) % QUAD
        return remote(gpart.at[g], gsum.at[q], g_send.at[step], g_recv.at[q], at(stage, g // 2, g % 2))

    def shared(step):
        g = (q + step) % QUAD
        return remote(gpart.at[g], gsum.at[g], g_send.at[step], g_recv.at[g], at(stage, g // 2, g % 2))

    for step in range(1, QUAD):
        share(step).start()
    vsum[stages - 1] = vsum[stages - 1] + gpart[q]
    for other in range(stages):
        @pl.when(((stage <= half) & (other > stage)) | ((stage > other) & (other > half)))
        def _():
            remote(rsum.at[other], rsum.at[other], r_send.at[0], r_recv.at[other],
                   at(stage, col, 1 - core)).wait_recv()
            vsum[stages - 1] = vsum[stages - 1] + rsum[other]

    for step in range(1, QUAD):
        shared(step).wait_recv()
        vsum[stages - 1] = vsum[stages - 1] + gsum[(q + step) % QUAD]
    mask = (tags[me] >= 0).astype(jnp.float32)
    out[...] = mask * base_weight / (vsum[stages - 1] + 1.0 - mask)

    def drain(k, _):
        @pl.when(stage <= half)
        def _():
            own_forward(k).wait_send()

        @pl.when(stage >= half + 2)
        def _():
            own_back(k).wait_send()

        across(q, k).wait_send()
        beside(q, k).wait_send()
        diagonal(q_across, k).wait_send()
        for s in range(half + 1):
            @pl.when((stage > s) & (stage < stages - 1))
            def _():
                pass_forward(s, k).wait_send()

            if s <= stages - 3 - half:
                @pl.when((stage >= half + 2) & (stage + s < stages - 1))
                def _():
                    pass_back(s, k).wait_send()
        return 0

    lax.fori_loop(0, chunks, drain, 0)

    def drain_tags(p, _):
        tag_copy(me, p, peer_of((me + p) % peers)).wait_send()
        return 0

    lax.fori_loop(1, peers, drain_tags, 0)
    each_return(lambda copy: copy.wait_send())
    for step in range(1, QUAD):
        share(step).wait_send()


def solution(mesh):
    stages = mesh.shape["blk"] // COLS

    def body(embeddings, cluster_ids, live_rows):
        rows, depth = embeddings.shape
        chunks = 4
        peers = stages * QUAD
        dma = pltpu.SemaphoreType.DMA
        f32 = jnp.float32
        weights = pl.pallas_call(
            functools.partial(kernel, stages, chunks),
            out_shape=jax.ShapeDtypeStruct((1, rows), f32),
            in_specs=[
                pl.BlockSpec(memory_space=pltpu.VMEM),
                pl.BlockSpec(memory_space=pltpu.VMEM),
                pl.BlockSpec(memory_space=pltpu.SMEM),
            ],
            out_specs=pl.BlockSpec(memory_space=pltpu.VMEM),
            scratch_shapes=[
                pltpu.VMEM((QUAD, rows, depth), jnp.bfloat16),
                pltpu.VMEM((stages - 1, rows, depth), jnp.bfloat16),
                pltpu.VMEM((peers, 1, rows), f32),
                pltpu.VMEM((QUAD, rows, 128), f32),
                pltpu.VMEM((QUAD, rows, 128), f32),
                pltpu.VMEM((QUAD, rows, 128), f32),
                pltpu.VMEM((stages, 1, rows), f32),
                pltpu.VMEM((stages, 1, rows), f32),
                pltpu.VMEM((QUAD, 1, rows), f32),
                pltpu.VMEM((QUAD, 1, rows), f32),
                dma((stages - 1, chunks)),
                dma((chunks,)),
                dma((stages - 1, chunks)),
                dma((chunks,)), dma((chunks,)),
                dma((chunks,)), dma((chunks,)),
                dma((chunks,)), dma((chunks,)),
                dma((peers,)), dma((peers,)),
                dma((stages - 1,)), dma((stages,)),
                dma((QUAD,)), dma((QUAD,)),
            ],
            compiler_params=pltpu.CompilerParams(
                collective_id=0, has_side_effects=True, vmem_limit_bytes=48 * 1024 * 1024
            ),
        )(embeddings, cluster_ids.reshape(1, rows), live_rows)
        return weights.reshape(rows)

    return jax.shard_map(
        body,
        mesh=mesh,
        in_specs=(
            P(("groups", "blk", "inner"), None),
            P(("groups", "blk", "inner")),
            P(("groups", "blk", "inner")),
        ),
        out_specs=P(("groups", "blk", "inner")),
        check_vma=False,
    )
```

time: 327 us -> 75.6 us (0.23)
  waiting for transfers between devices: 239 us -> 0 us
  Pallas kernels: 0 us -> 73 us
  matrix products: 25.9 us -> 0 us
  local copies, waits for them, and re-layouts: 16.9 us -> 1.82 us
  blocking collectives: 14.3 us -> 0 us
  between operations: 14.1 us -> 0.68 us
  starting transfers between devices: 11.4 us -> 0 us
  other arithmetic: 4.71 us -> 0 us
    ppermute x14 -> x0, waiting for transfers between devices: 229 us -> none  [from_behind(): return lax.ppermute(block, axis, route)]
    pallas_call x0 -> x1, Pallas kernels: none -> 73 us  [body(): pl.pallas_call(functools.partial(kernel, stages, chunks), out_shape=jax.S...]
    dot_general x8 -> x0, matrix products: 25.9 us -> none  [kernel_tile(): lax.dot_general(unit_rows, visible_rows, (((1,), (1,)), ((), ())), prefer...]
    while x28 -> x0, local copies, waits for them, and re-layouts: 15.5 us -> none
    all_gather x8 -> x0, blocking collectives: 14.3 us -> none  [widen_block(): lax.all_gather(as_sent(visitor), 'inner', axis=0, tiled=True)]
    ppermute x14 -> x0, starting transfers between devices: 11.1 us -> none  [from_behind(): return lax.ppermute(block, axis, route)]
    all_gather x8 -> x0, waiting for transfers between devices: 9.51 us -> none  [widen_block(): lax.all_gather(as_sent(visitor), 'inner', axis=0, tiled=True)]
  transfers between devices with their start and end apart: 22 -> 0, of which waited for: 15 -> 0; matrix products, arithmetic and copies ran while one was open for 3% -> 0% of each run, Pallas kernels for 0% -> 0%
where the time goes in v1:
time: 75.6 us; the launch traced here: 75.5 us
  Pallas kernels  73 us (97%)
  local copies, waits for them, and re-layouts  1.82 us (2%)
    pallas_call x1, Pallas kernels, body(): pl.pallas_call(functools.partial(kernel, stages, chunks), out_shape=jax.S...  73 us
    unnamed x5, local copies, waits for them, and re-layouts  1.82 us

profile of v1, /device:TPU:0, one launch (start us, length us, event | category | flops | bytes accessed | tf_op | source)
XLA Modules:
  0.0 75.5 jit_solution(13681988044088471180)
XLA Ops:
  0.0 0.0 copy-start.1
  0.7 0.0 copy-done.1
  0.7 0.0 copy-start
  0.7 1.2 %copy-done = bf16[512,1024]{1,0:T(8,128)(2,1)S(1)} copy-done((bf16[512,1024]{1,0:T(8,128)(2,1)S(1)}, bf16[512,1024]{1,0:T(8,128)(2,1)}, u32[]{:S(2)}) %copy-start) | copy-done | bytes 1048600
  1.9 73.0 %shard_map.37 = f32[1,512]{1,0:T(1,128)S(1)} custom-call(bf16[512,1024]{1,0:T(8,128)(2,1)S(1)} %copy-done, s32[1,512]{1,0:T(1,128)S(1)} %bitcast.3, s32[1]{0:T(128)S(6)} %copy.5.live), custom_call_target="tpu_custom_call" | custom-call | tf_op jit(solution)/shard_map/pallas_call | solution.py:323
  74.9 0.6 copy.6
Async XLA Ops:
  0.0 0.7 copy-start.1
  0.7 1.2 %copy-start = (bf16[512,1024]{1,0:T(8,128)(2,1)S(1)}, bf16[512,1024]{1,0:T(8,128)(2,1)}, u32[]{:S(2)}) copy-start(bf16[512,1024]{1,0:T(8,128)(2,1)} %emb.1) | copy-start | bytes 3145732

commit v2 on v1

--- a/solution.py
+++ b/solution.py
@@ -19,23 +19,29 @@
 
 
 def kernel(
-    stages, chunks, emb, ids, live, out,
-    quad, vis, tags, tag_col, cap_col, acc, vsum, rsum, gpart, gsum,
+    stages, chunks, detour, emb, ids, live, out,
+    quad, vis, relay_rows, tags, tag_col, cap_col, acc, vsum, rsum, gpart, gsum,
     fwd_send, own_send, vis_recv, y_send, y_recv, i_send, i_recv, d_send, d_recv,
-    t_send, t_recv, r_send, r_recv, g_send, g_recv,
+    x_recv, o_send, h_send, t_send, t_recv, r_send, r_recv, g_send, g_recv,
 ):
     rows, depth = emb.shape
     span = rows // chunks
     half = stages // 2 - 1
     blk, core = lax.axis_index("blk"), lax.axis_index("inner")
-    stage, col = blk // COLS, blk % COLS
+    odd = lax.axis_index("groups") % 2 if detour else 0
+    group = lax.axis_index("groups")
+
+    def flip(s):
+        return s + odd * (stages - 1 - 2 * s)
+
+    stage, col = flip(blk // COLS), blk % COLS
     upper = stage // (half + 1)
     q = col * 2 + core
     me = blk * 2 + core
     peers = stages * QUAD
 
     def at(s, y, c):
-        return {"blk": s * COLS + y, "inner": c}
+        return {"blk": flip(s) * COLS + y, "inner": c}
 
     def peer_of(index):
         return {"blk": index // 2, "inner": index % 2}
@@ -83,6 +89,37 @@
         return remote(quad.at[owner, part(k)], quad.at[owner, part(k)], d_send.at[k], d_recv.at[k],
                       at(stage, col, 1 - core))
 
+    twin = {"groups": group + 1 - 2 * odd}
+
+    def relay_in(k):
+        return remote(vis.at[0, part(k)], relay_rows.at[part(k)], fwd_send.at[0, k], x_recv.at[k], twin)
+
+    def relay_on(k):
+        return remote(relay_rows.at[part(k)], relay_rows.at[part(k)], o_send.at[k], x_recv.at[k],
+                      at(stage - 1, col, core))
+
+    def relay_home(k):
+        return remote(relay_rows.at[part(k)], vis.at[1, part(k)], h_send.at[k], vis_recv.at[1, k], twin)
+
+    def relay_arrival(k):
+        return remote(relay_rows.at[part(k)], relay_rows.at[part(k)], o_send.at[k], x_recv.at[k], twin)
+
+    def carry(k):
+        if k >= detour:
+            return
+
+        @pl.when(stage < stages - 1)
+        def _():
+            relay_arrival(k).wait_recv()
+
+            @pl.when(stage < 2)
+            def _():
+                relay_home(k).start()
+
+            @pl.when(stage > 0)
+            def _():
+                relay_on(k).start()
+
     def tag_copy(owner, sem, device):
         return remote(tags.at[owner], tags.at[owner], t_send.at[sem], t_recv.at[owner], device)
 
@@ -96,6 +133,8 @@
         return 0
 
     lax.fori_loop(1, peers, greet, 0)
+    if detour:
+        pl.semaphore_signal(barrier, inc=1, device_id=twin, device_id_type=MESH)
 
     def normalize(k):
         wide = emb[part(k), :].astype(jnp.float32)
@@ -105,7 +144,7 @@
     position = lax.broadcasted_iota(jnp.int32, (1, rows), 1)
     tags[me] = jnp.where(position < live[0], ids[...], -1).astype(jnp.float32)
     normalize(0)
-    pl.semaphore_wait(barrier, peers - 1)
+    pl.semaphore_wait(barrier, peers - 1 + (1 if detour else 0))
 
     def start_own(k):
         @pl.when(stage <= half)
@@ -138,9 +177,20 @@
         def _():
             arrival(s, k).wait_recv()
 
-            @pl.when(stage < stages - 1)
-            def _():
-                pass_forward(s, k).start()
+            if s == 0 and k < detour:
+                @pl.when(stage == 1)
+                def _():
+                    relay_in(k).start()
+
+                @pl.when(stage == 2)
+                def _():
+                    pass_forward(s, k).start()
+            elif s > 0 and k < detour:
+                pass
+            else:
+                @pl.when(stage < stages - 1)
+                def _():
+                    pass_forward(s, k).start()
 
         if s <= stages - 3 - half:
             @pl.when((stage > half) & (stage + s < stages - 1))
@@ -151,13 +201,12 @@
                 def _():
                     pass_back(s, k).start()
 
-    def first(k, _):
+    for k in range(chunks):
         receive(0, k)
         across(q_across, k).wait_recv()
         diagonal(q_across, k).start()
-        return 0
-
-    lax.fori_loop(0, chunks, first, 0)
+        if k % 2 == 0 and k > 0:
+            carry(k // 2 - 1)
 
     def take_tags(p, _):
         tag_copy((me + p) % peers, p, peer_of((me + p) % peers)).wait_recv()
@@ -165,7 +214,7 @@
 
     lax.fori_loop(1, peers, take_tags, 0)
     for g in range(QUAD):
-        row = tags[stage * QUAD + g]
+        row = tags[flip(stage) * QUAD + g]
         tall = jnp.broadcast_to(row, (128, rows)).T
         tag_col[g] = tall
         cap_col[g] = jnp.where(tall < 0, NEG, 0.0)
@@ -178,56 +227,85 @@
 
     lax.fori_loop(0, chunks, settle, 0)
 
-    def visit(block, owner, slot, k, keep):
-        seen = block[part(k), :]
-        lanes = pl.ds(pl.multiple_of(k * span, span), span)
+    unit = rows // 2
+
+    def visit(block, owner, slot, u, keep):
+        lanes = slice(u * unit, (u + 1) * unit)
+        seen = block[lanes, :]
         tag_row = tags[owner, :, lanes]
         same = jnp.where(tag_row < 0, NEG, -sharpness * LOG2E)
         other = same - 2.0
-
-        def tile(g, total):
-            cosines = lax.dot_general(
-                quad[g], seen, (((1,), (1,)), ((), ())), preferred_element_type=jnp.float32
-            )
-            bias = jnp.where(tag_col[g] == tag_row, same, other) + cap_col[g]
-            weight = jnp.exp2(cosines * (sharpness * LOG2E) + bias)
-            if keep:
-                acc[g] += weight
-            return total + jnp.sum(weight.reshape(rows // 8, 8, span), axis=0)
-
-        total = lax.fori_loop(0, QUAD, tile, jnp.zeros((8, span), jnp.float32))
+        total = jnp.zeros((8, unit), jnp.float32)
+        tall = rows // 2
+        for g in range(QUAD):
+            for t in range(rows // tall):
+                down = slice(t * tall, (t + 1) * tall)
+                cosines = lax.dot_general(
+                    quad[g, down, :], seen, (((1,), (1,)), ((), ())),
+                    preferred_element_type=jnp.float32,
+                )
+                scaled = cosines * (sharpness * LOG2E)
+                kept = acc[g, down, :] if keep else None
+                sums = []
+                for b in range(unit // 128):
+                    wide = slice(b * 128, (b + 1) * 128)
+                    bias = jnp.where(tag_col[g, down, :] == tag_row[:, wide], same[:, wide], other[:, wide])
+                    weight = jnp.exp2(scaled[:, wide] + (bias + cap_col[g, down, :]))
+                    if keep:
+                        kept = kept + weight
+                    sums.append(jnp.sum(weight.reshape(tall // 8, 8, 128), axis=0))
+                if keep:
+                    acc[g, down, :] = kept
+                total = total + jnp.concatenate(sums, axis=1)
         vsum[slot, :, lanes] = jnp.sum(total, axis=0, keepdims=True)
 
     def owner_of(visitor):
-        return visitor * QUAD + q
-
-    def visit_forward(s, k):
-        @pl.when((stage > s) & (stage <= half))
-        def _():
-            visit(vis.at[s], owner_of(stage - 1 - s), s, k, True)
-
-        @pl.when(stage > half)
-        def _():
-            visit(vis.at[s], owner_of(half - s), s, k, True)
-
-    def visit_back(s, k):
+        return flip(visitor) * QUAD + q
+
+    def from_below(s):
+        return (stage - 1) * (1 - upper) + half * upper - s
+
+    def visit_forward(s, u):
+        @pl.when(stage > s)
+        def _():
+            visit(vis.at[s], owner_of(from_below(s)), s, u, True)
+
+    def visit_back(s, u):
         if s <= stages - 3 - half:
             @pl.when((stage > half) & (stage + s < stages - 1))
             def _():
-                visit(vis.at[half + 1 + s], owner_of(stage + 1 + s), half + 1 + s, k, True)
-
-    for s in range(1, half + 1):
-        def turn(k, _):
-            if s == 1:
-                visit(quad.at[q], me, stages - 1, k, False)
-                visit_forward(0, k)
-                visit_back(0, k)
-            receive(s, k)
-            visit_forward(s, k)
-            visit_back(s, k)
-            return 0
-
-        lax.fori_loop(0, chunks, turn, 0)
+                visit(vis.at[half + 1 + s], owner_of(stage + 1 + s), half + 1 + s, u, True)
+
+    def visit_own(u):
+        visit(quad.at[q], me, stages - 1, u, False)
+
+    early = chunks // 2 + 1
+    carry(3)
+    visit_own(0)
+    carry(4)
+    visit_forward(0, 0)
+    visit_back(0, 0)
+    for k in range(5, detour):
+        carry(k)
+    for k in range(early):
+        receive(1, k)
+    visit_forward(1, 0)
+    visit_back(1, 0)
+    receive(1, early)
+    visit_own(1)
+    visit_forward(0, 1)
+    for k in range(early + 1, chunks - 1):
+        receive(1, k)
+    visit_back(0, 1)
+    receive(1, chunks - 1)
+    visit_forward(1, 1)
+    visit_back(1, 1)
+    for s in range(2, half + 1):
+        for u in range(2):
+            for k in range(u * chunks // 2, (u + 1) * chunks // 2):
+                receive(s, k)
+            visit_forward(s, u)
+            visit_back(s, u)
 
     def give_back(slot, visitor):
         return remote(vsum.at[slot], rsum.at[stage], r_send.at[slot], r_recv.at[stage],
@@ -235,13 +313,9 @@
 
     def each_return(act):
         for s in range(half + 1):
-            @pl.when((stage > s) & (stage <= half))
-            def _():
-                act(give_back(s, stage - 1 - s))
-
-            @pl.when(stage > half)
-            def _():
-                act(give_back(s, half - s))
+            @pl.when(stage > s)
+            def _():
+                act(give_back(s, from_below(s)))
 
             if s <= stages - 3 - half:
                 @pl.when((stage > half) & (stage + s < stages - 1))
@@ -276,7 +350,7 @@
     mask = (tags[me] >= 0).astype(jnp.float32)
     out[...] = mask * base_weight / (vsum[stages - 1] + 1.0 - mask)
 
-    def drain(k, _):
+    for k in range(chunks):
         @pl.when(stage <= half)
         def _():
             own_forward(k).wait_send()
@@ -289,17 +363,29 @@
         beside(q, k).wait_send()
         diagonal(q_across, k).wait_send()
         for s in range(half + 1):
-            @pl.when((stage > s) & (stage < stages - 1))
-            def _():
-                pass_forward(s, k).wait_send()
+            if s == 0 and k < detour:
+                @pl.when((stage == 1) | (stage == 2))
+                def _():
+                    pass_forward(s, k).wait_send()
+            elif s > 0 and k < detour:
+                pass
+            else:
+                @pl.when((stage > s) & (stage < stages - 1))
+                def _():
+                    pass_forward(s, k).wait_send()
 
             if s <= stages - 3 - half:
                 @pl.when((stage >= half + 2) & (stage + s < stages - 1))
                 def _():
                     pass_back(s, k).wait_send()
-        return 0
-
-    lax.fori_loop(0, chunks, drain, 0)
+        if k < detour:
+            @pl.when(stage < 2)
+            def _():
+                relay_home(k).wait_send()
+
+            @pl.when((stage > 0) & (stage < stages - 1))
+            def _():
+                relay_on(k).wait_send()
 
     def drain_tags(p, _):
         tag_copy(me, p, peer_of((me + p) % peers)).wait_send()
@@ -316,12 +402,13 @@
 
     def body(embeddings, cluster_ids, live_rows):
         rows, depth = embeddings.shape
-        chunks = 4
+        chunks = 8
+        detour = 5 if stages == 4 and mesh.shape["groups"] % 2 == 0 else 0
         peers = stages * QUAD
         dma = pltpu.SemaphoreType.DMA
         f32 = jnp.float32
         weights = pl.pallas_call(
-            functools.partial(kernel, stages, chunks),
+            functools.partial(kernel, stages, chunks, detour),
             out_shape=jax.ShapeDtypeStruct((1, rows), f32),
             in_specs=[
                 pl.BlockSpec(memory_space=pltpu.VMEM),
@@ -332,6 +419,7 @@
             scratch_shapes=[
                 pltpu.VMEM((QUAD, rows, depth), jnp.bfloat16),
                 pltpu.VMEM((stages - 1, rows, depth), jnp.bfloat16),
+                pltpu.VMEM((rows, depth), jnp.bfloat16),
                 pltpu.VMEM((peers, 1, rows), f32),
                 pltpu.VMEM((QUAD, rows, 128), f32),
                 pltpu.VMEM((QUAD, rows, 128), f32),
@@ -346,6 +434,7 @@
                 dma((chunks,)), dma((chunks,)),
                 dma((chunks,)), dma((chunks,)),
                 dma((chunks,)), dma((chunks,)),
+                dma((chunks,)), dma((chunks,)), dma((chunks,)),
                 dma((peers,)), dma((peers,)),
                 dma((stages - 1,)), dma((stages,)),
                 dma((QUAD,)), dma((QUAD,)),

time: 75.6 us -> 66.2 us (0.88)
  Pallas kernels: 73 us -> 63.5 us
    pallas_call x1, Pallas kernels: 73 us -> 63.5 us  [body(): pl.pallas_call(functools.partial(kernel, stages, chunks, detour), out_sha...]
where the time goes in v2:
time: 66.2 us; the launch traced here: 66 us
  Pallas kernels  63.5 us (96%)
  local copies, waits for them, and re-layouts  1.82 us (3%)
  between operations  0.68 us (1%)
    pallas_call x1, Pallas kernels, body(): pl.pallas_call(functools.partial(kernel, stages, chunks, detour), out_sha...  63.5 us
    unnamed x5, local copies, waits for them, and re-layouts  1.82 us

profile of v2, /device:TPU:0, one launch (start us, length us, event | category | flops | bytes accessed | tf_op | source)
XLA Modules:
  0.0 66.0 jit_solution(15419371285124593000)
XLA Ops:
  0.0 0.0 copy-start.1
  0.7 0.0 copy-done.1
  0.7 0.0 copy-start
  0.7 1.2 %copy-done = bf16[512,1024]{1,0:T(8,128)(2,1)S(1)} copy-done((bf16[512,1024]{1,0:T(8,128)(2,1)S(1)}, bf16[512,1024]{1,0:T(8,128)(2,1)}, u32[]{:S(2)}) %copy-start) | copy-done | bytes 1048600
  1.9 63.5 %shard_map.37 = f32[1,512]{1,0:T(1,128)S(1)} custom-call(bf16[512,1024]{1,0:T(8,128)(2,1)S(1)} %copy-done, s32[1,512]{1,0:T(1,128)S(1)} %bitcast.3, s32[1]{0:T(128)S(6)} %copy.5.live), custom_call_target="tpu_custom_call" | custom-call | tf_op jit(solution)/shard_map/pallas_call | solution.py:410
  65.4 0.6 copy.6
Async XLA Ops:
  0.0 0.7 %copy-start.1 = (s32[512]{0:T(512)S(1)}, s32[512]{0:T(512)}, u32[]{:S(2)}) copy-start(s32[512]{0:T(512)} %param.4) | copy-start | bytes 6148
  0.7 1.2 %copy-start = (bf16[512,1024]{1,0:T(8,128)(2,1)S(1)}, bf16[512,1024]{1,0:T(8,128)(2,1)}, u32[]{:S(2)}) copy-start(bf16[512,1024]{1,0:T(8,128)(2,1)} %emb.1) | copy-start | bytes 3145732

commit v3 on v2

--- a/solution.py
+++ b/solution.py
@@ -20,7 +20,7 @@
 
 def kernel(
     stages, chunks, detour, emb, ids, live, out,
-    quad, vis, relay_rows, tags, tag_col, cap_col, acc, vsum, rsum, gpart, gsum,
+    staged, e_sem, quad, vis, relay_rows, tags, tag_col, cap_col, acc, vsum, rsum, gpart, gsum,
     fwd_send, own_send, vis_recv, y_send, y_recv, i_send, i_recv, d_send, d_recv,
     x_recv, o_send, h_send, t_send, t_recv, r_send, r_recv, g_send, g_recv,
 ):
@@ -104,11 +104,11 @@
     def relay_arrival(k):
         return remote(relay_rows.at[part(k)], relay_rows.at[part(k)], o_send.at[k], x_recv.at[k], twin)
 
-    def carry(k):
-        if k >= detour:
+    def carry(k, role):
+        if k < 0 or k >= detour:
             return
 
-        @pl.when(stage < stages - 1)
+        @pl.when(stage == role)
         def _():
             relay_arrival(k).wait_recv()
 
@@ -126,6 +126,11 @@
     q_across, q_beside = (1 - col) * 2 + core, col * 2 + 1 - core
     q_diag = (1 - col) * 2 + 1 - core
 
+    def load(k):
+        return pltpu.make_async_copy(emb.at[part(k)], staged.at[part(k)], e_sem.at[k])
+
+    for k in range(chunks):
+        load(k).start()
     barrier = pltpu.get_barrier_semaphore()
 
     def greet(p, _):
@@ -137,7 +142,8 @@
         pl.semaphore_signal(barrier, inc=1, device_id=twin, device_id_type=MESH)
 
     def normalize(k):
-        wide = emb[part(k), :].astype(jnp.float32)
+        load(k).wait()
+        wide = staged[part(k), :].astype(jnp.float32)
         scale = lax.rsqrt(jnp.mean(wide * wide, axis=1, keepdims=True) + epsilon) / math.sqrt(depth)
         quad[q, part(k), :] = (wide * scale).astype(jnp.bfloat16)
 
@@ -201,25 +207,29 @@
                 def _():
                     pass_back(s, k).start()
 
-    for k in range(chunks):
-        receive(0, k)
-        across(q_across, k).wait_recv()
-        diagonal(q_across, k).start()
-        if k % 2 == 0 and k > 0:
-            carry(k // 2 - 1)
-
     def take_tags(p, _):
         tag_copy((me + p) % peers, p, peer_of((me + p) % peers)).wait_recv()
         return 0
 
-    lax.fori_loop(1, peers, take_tags, 0)
-    for g in range(QUAD):
+    def lay_tags(g):
         row = tags[flip(stage) * QUAD + g]
         tall = jnp.broadcast_to(row, (128, rows)).T
         tag_col[g] = tall
         cap_col[g] = jnp.where(tall < 0, NEG, 0.0)
         acc[g] = jnp.zeros((rows, 128), jnp.float32)
 
+    for k in range(chunks):
+        if k == 2:
+            lax.fori_loop(1, peers, take_tags, 0)
+        if 2 <= k < 2 + QUAD:
+            lay_tags(k - 2)
+        receive(0, k)
+        across(q_across, k).wait_recv()
+        diagonal(q_across, k).start()
+        carry(k - 1, 2)
+        carry(k - 2, 1)
+        carry(k - 3, 0)
+
     def settle(k, _):
         beside(q_beside, k).wait_recv()
         diagonal(q_diag, k).wait_recv()
@@ -227,10 +237,13 @@
 
     lax.fori_loop(0, chunks, settle, 0)
 
-    unit = rows // 2
+    third = rows // 2 + rows // 4
+    bounds = {0: (0, rows // 2), 1: (rows // 2, rows), 2: (rows // 2, third), 3: (third, rows)}
 
     def visit(block, owner, slot, u, keep):
-        lanes = slice(u * unit, (u + 1) * unit)
+        low, high = bounds[u]
+        unit = high - low
+        lanes = slice(low, high)
         seen = block[lanes, :]
         tag_row = tags[owner, :, lanes]
         same = jnp.where(tag_row < 0, NEG, -sharpness * LOG2E)
@@ -279,27 +292,38 @@
     def visit_own(u):
         visit(quad.at[q], me, stages - 1, u, False)
 
-    early = chunks // 2 + 1
-    carry(3)
+    for k in range(chunks, chunks + 3):
+        carry(k - 1, 2)
+        carry(k - 2, 1)
+        carry(k - 3, 0)
     visit_own(0)
-    carry(4)
+    direct = list(range(detour, chunks)) if detour else []
+    waiting = [k for k in range(chunks) if k not in direct]
+    for k in direct[:1]:
+        receive(1, k)
     visit_forward(0, 0)
     visit_back(0, 0)
-    for k in range(5, detour):
-        carry(k)
-    for k in range(early):
+    for k in direct[1:2]:
+        receive(1, k)
+    for k in waiting[:chunks // 2]:
         receive(1, k)
     visit_forward(1, 0)
     visit_back(1, 0)
-    receive(1, early)
     visit_own(1)
     visit_forward(0, 1)
-    for k in range(early + 1, chunks - 1):
+    for k in direct[2:]:
         receive(1, k)
     visit_back(0, 1)
-    receive(1, chunks - 1)
-    visit_forward(1, 1)
-    visit_back(1, 1)
+    for k in waiting[chunks // 2:]:
+        if k < third // span:
+            receive(1, k)
+    visit_forward(1, 2)
+    visit_back(1, 2)
+    for k in waiting[chunks // 2:]:
+        if k >= third // span:
+            receive(1, k)
+    visit_forward(1, 3)
+    visit_back(1, 3)
     for s in range(2, half + 1):
         for u in range(2):
             for k in range(u * chunks // 2, (u + 1) * chunks // 2):
@@ -411,12 +435,14 @@
             functools.partial(kernel, stages, chunks, detour),
             out_shape=jax.ShapeDtypeStruct((1, rows), f32),
             in_specs=[
-                pl.BlockSpec(memory_space=pltpu.VMEM),
+                pl.BlockSpec(memory_space=pl.ANY),
                 pl.BlockSpec(memory_space=pltpu.VMEM),
                 pl.BlockSpec(memory_space=pltpu.SMEM),
             ],
             out_specs=pl.BlockSpec(memory_space=pltpu.VMEM),
             scratch_shapes=[
+                pltpu.VMEM((rows, depth), jnp.bfloat16),
+                dma((chunks,)),
                 pltpu.VMEM((QUAD, rows, depth), jnp.bfloat16),
                 pltpu.VMEM((stages - 1, rows, depth), jnp.bfloat16),
                 pltpu.VMEM((rows, depth), jnp.bfloat16),

time: 66.2 us -> 60.4 us (0.912)
  Pallas kernels: 63.5 us -> 57.7 us
    pallas_call x1, Pallas kernels: 63.5 us -> 57.7 us  [body(): pl.pallas_call(functools.partial(kernel, stages, chunks, detour), out_sha...]
where the time goes in v3:
time: 60.4 us; the launch traced here: 60.2 us
  Pallas kernels  57.7 us (96%)
  local copies, waits for them, and re-layouts  1.82 us (3%)
  between operations  0.68 us (1%)
    pallas_call x1, Pallas kernels, body(): pl.pallas_call(functools.partial(kernel, stages, chunks, detour), out_sha...  57.7 us
    unnamed x5, local copies, waits for them, and re-layouts  1.82 us

profile of v3, /device:TPU:0, one launch (start us, length us, event | category | flops | bytes accessed | tf_op | source)
XLA Modules:
  0.0 60.2 jit_solution(9470165066676660423)
XLA Ops:
  0.0 0.0 copy-start.1
  0.7 0.0 copy-done.1
  0.7 0.0 copy-start
  0.7 1.2 %copy-done = bf16[512,1024]{1,0:T(8,128)(2,1)S(1)} copy-done((bf16[512,1024]{1,0:T(8,128)(2,1)S(1)}, bf16[512,1024]{1,0:T(8,128)(2,1)}, u32[]{:S(2)}) %copy-start) | copy-done | bytes 1048600
  1.9 57.7 %shard_map.37 = f32[1,512]{1,0:T(1,128)S(1)} custom-call(bf16[512,1024]{1,0:T(8,128)(2,1)S(1)} %copy-done, s32[1,512]{1,0:T(1,128)S(1)} %bitcast.3, s32[1]{0:T(128)S(6)} %copy.5.live), custom_call_target="tpu_custom_call" | custom-call | tf_op jit(solution)/shard_map/pallas_call | solution.py:434
  59.6 0.6 copy.6
Async XLA Ops:
  0.0 0.7 %copy-start.1 = (s32[512]{0:T(512)S(1)}, s32[512]{0:T(512)}, u32[]{:S(2)}) copy-start(s32[512]{0:T(512)} %param.4) | copy-start | bytes 6148
  0.7 1.2 %copy-start = (bf16[512,1024]{1,0:T(8,128)(2,1)S(1)}, bf16[512,1024]{1,0:T(8,128)(2,1)}, u32[]{:S(2)}) copy-start(bf16[512,1024]{1,0:T(8,128)(2,1)} %emb.1) | copy-start | bytes 3145732

commit v4 on v3

--- a/solution.py
+++ b/solution.py
@@ -22,7 +22,7 @@
     stages, chunks, detour, emb, ids, live, out,
     staged, e_sem, quad, vis, relay_rows, tags, tag_col, cap_col, acc, vsum, rsum, gpart, gsum,
     fwd_send, own_send, vis_recv, y_send, y_recv, i_send, i_recv, d_send, d_recv,
-    x_recv, o_send, h_send, t_send, t_recv, r_send, r_recv, g_send, g_recv,
+    n_send, x_recv, o_send, h_send, t_send, t_recv, r_send, r_recv, g_send, g_recv,
 ):
     rows, depth = emb.shape
     span = rows // chunks
@@ -89,10 +89,14 @@
         return remote(quad.at[owner, part(k)], quad.at[owner, part(k)], d_send.at[k], d_recv.at[k],
                       at(stage, col, 1 - core))
 
+    entering = 2 if detour else 0
     twin = {"groups": group + 1 - 2 * odd}
 
     def relay_in(k):
         return remote(vis.at[0, part(k)], relay_rows.at[part(k)], fwd_send.at[0, k], x_recv.at[k], twin)
+
+    def relay_enter(k):
+        return remote(quad.at[q, part(k)], relay_rows.at[part(k)], n_send.at[k], x_recv.at[k], twin)
 
     def relay_on(k):
         return remote(relay_rows.at[part(k)], relay_rows.at[part(k)], o_send.at[k], x_recv.at[k],
@@ -161,6 +165,11 @@
         def _():
             own_back(k).start()
 
+        if detour:
+            @pl.when((stage == 0) & (k < entering))
+            def _():
+                relay_enter(k).start()
+
         across(q, k).start()
         beside(q, k).start()
 
@@ -184,9 +193,10 @@
             arrival(s, k).wait_recv()
 
             if s == 0 and k < detour:
-                @pl.when(stage == 1)
-                def _():
-                    relay_in(k).start()
+                if k >= entering:
+                    @pl.when(stage == 1)
+                    def _():
+                        relay_in(k).start()
 
                 @pl.when(stage == 2)
                 def _():
@@ -223,6 +233,8 @@
             lax.fori_loop(1, peers, take_tags, 0)
         if 2 <= k < 2 + QUAD:
             lay_tags(k - 2)
+        if k < entering:
+            carry(k, 3)
         receive(0, k)
         across(q_across, k).wait_recv()
         diagonal(q_across, k).start()
@@ -388,7 +400,7 @@
         diagonal(q_across, k).wait_send()
         for s in range(half + 1):
             if s == 0 and k < detour:
-                @pl.when((stage == 1) | (stage == 2))
+                @pl.when(((stage == 1) & (k >= entering)) | (stage == 2))
                 def _():
                     pass_forward(s, k).wait_send()
             elif s > 0 and k < detour:
@@ -407,9 +419,13 @@
             def _():
                 relay_home(k).wait_send()
 
-            @pl.when((stage > 0) & (stage < stages - 1))
+            @pl.when((stage > 0) & ((stage < stages - 1) | (k < entering)))
             def _():
                 relay_on(k).wait_send()
+
+            @pl.when((stage == 0) & (k < entering))
+            def _():
+                relay_enter(k).wait_send()
 
     def drain_tags(p, _):
         tag_copy(me, p, peer_of((me + p) % peers)).wait_send()
@@ -427,7 +443,7 @@
     def body(embeddings, cluster_ids, live_rows):
         rows, depth = embeddings.shape
         chunks = 8
-        detour = 5 if stages == 4 and mesh.shape["groups"] % 2 == 0 else 0
+        detour = 6 if stages == 4 and mesh.shape["groups"] % 2 == 0 else 0
         peers = stages * QUAD
         dma = pltpu.SemaphoreType.DMA
         f32 = jnp.float32
@@ -460,7 +476,7 @@
                 dma((chunks,)), dma((chunks,)),
                 dma((chunks,)), dma((chunks,)),
                 dma((chunks,)), dma((chunks,)),
-                dma((chunks,)), dma((chunks,)), dma((chunks,)),
+                dma((chunks,)), dma((chunks,)), dma((chunks,)), dma((chunks,)),
                 dma((peers,)), dma((peers,)),
                 dma((stages - 1,)), dma((stages,)),
                 dma((QUAD,)), dma((QUAD,)),

time: 60.4 us -> 83 us (1.37)
  Pallas kernels: 57.7 us -> 80.3 us
    pallas_call x1, Pallas kernels: 57.7 us -> 80.3 us  [body(): pl.pallas_call(functools.partial(kernel, stages, chunks, detour), out_sha...]
where the time goes in v4:
time: 83 us; the launch traced here: 82.8 us
  Pallas kernels  80.3 us (97%)
  local copies, waits for them, and re-layouts  1.82 us (2%)
    pallas_call x1, Pallas kernels, body(): pl.pallas_call(functools.partial(kernel, stages, chunks, detour), out_sha...  80.3 us
    unnamed x5, local copies, waits for them, and re-layouts  1.82 us

profile of v4, /device:TPU:0, one launch (start us, length us, event | category | flops | bytes accessed | tf_op | source)
XLA Modules:
  0.0 82.8 jit_solution(16209484847807339123)
XLA Ops:
  0.0 0.0 copy-start.1
  0.7 0.0 copy-done.1
  0.7 0.0 copy-start
  0.7 1.2 %copy-done = bf16[512,1024]{1,0:T(8,128)(2,1)S(1)} copy-done((bf16[512,1024]{1,0:T(8,128)(2,1)S(1)}, bf16[512,1024]{1,0:T(8,128)(2,1)}, u32[]{:S(2)}) %copy-start) | copy-done | bytes 1048600
  1.9 80.3 %shard_map.37 = f32[1,512]{1,0:T(1,128)S(1)} custom-call(bf16[512,1024]{1,0:T(8,128)(2,1)S(1)} %copy-done, s32[1,512]{1,0:T(1,128)S(1)} %bitcast.3, s32[1]{0:T(128)S(6)} %copy.5.live), custom_call_target="tpu_custom_call" | custom-call | tf_op jit(solution)/shard_map/pallas_call | solution.py:450
  82.2 0.6 copy.6
Async XLA Ops:
  0.0 0.7 copy-start.1
  0.7 1.2 %copy-start = (bf16[512,1024]{1,0:T(8,128)(2,1)S(1)}, bf16[512,1024]{1,0:T(8,128)(2,1)}, u32[]{:S(2)}) copy-start(bf16[512,1024]{1,0:T(8,128)(2,1)} %emb.1) | copy-start | bytes 3145732

commit v5 on v3

--- a/solution.py
+++ b/solution.py
@@ -224,11 +224,11 @@
         if 2 <= k < 2 + QUAD:
             lay_tags(k - 2)
         receive(0, k)
-        across(q_across, k).wait_recv()
-        diagonal(q_across, k).start()
         carry(k - 1, 2)
         carry(k - 2, 1)
         carry(k - 3, 0)
+        across(q_across, k).wait_recv()
+        diagonal(q_across, k).start()
 
     def settle(k, _):
         beside(q_beside, k).wait_recv()

time: 60.4 us -> 60.4 us (level)
  no operation moved by 1% of the time
where the time goes in v5:
time: 60.4 us; the launch traced here: 60.2 us
  Pallas kernels  57.7 us (96%)
  local copies, waits for them, and re-layouts  1.82 us (3%)
  between operations  0.68 us (1%)
    pallas_call x1, Pallas kernels, body(): pl.pallas_call(functools.partial(kernel, stages, chunks, detour), out_sha...  57.7 us
    unnamed x5, local copies, waits for them, and re-layouts  1.82 us

profile of v5, /device:TPU:0, one launch (start us, length us, event | category | flops | bytes accessed | tf_op | source)
XLA Modules:
  0.0 60.2 jit_solution(3215846316104577889)
XLA Ops:
  0.0 0.0 copy-start.1
  0.7 0.0 copy-done.1
  0.7 0.0 copy-start
  0.7 1.2 %copy-done = bf16[512,1024]{1,0:T(8,128)(2,1)S(1)} copy-done((bf16[512,1024]{1,0:T(8,128)(2,1)S(1)}, bf16[512,1024]{1,0:T(8,128)(2,1)}, u32[]{:S(2)}) %copy-start) | copy-done | bytes 1048600
  1.9 57.7 %shard_map.37 = f32[1,512]{1,0:T(1,128)S(1)} custom-call(bf16[512,1024]{1,0:T(8,128)(2,1)S(1)} %copy-done, s32[1,512]{1,0:T(1,128)S(1)} %bitcast.3, s32[1]{0:T(128)S(6)} %copy.5.live), custom_call_target="tpu_custom_call" | custom-call | tf_op jit(solution)/shard_map/pallas_call | solution.py:434
  59.6 0.6 copy.6
Async XLA Ops:
  0.0 0.7 %copy-start.1 = (s32[512]{0:T(512)S(1)}, s32[512]{0:T(512)}, u32[]{:S(2)}) copy-start(s32[512]{0:T(512)} %param.4) | copy-start | bytes 6148
  0.7 1.2 %copy-start = (bf16[512,1024]{1,0:T(8,128)(2,1)S(1)}, bf16[512,1024]{1,0:T(8,128)(2,1)}, u32[]{:S(2)}) copy-start(bf16[512,1024]{1,0:T(8,128)(2,1)} %emb.1) | copy-start | bytes 3145732
